TPU v7x, 32 devices: a whole 2x2x4 slice. The times are simulated.
32 devices in a mesh: groups: 2 (over x), rows: 8 (over z, y), cols: 2 (over core).
Axes of the slice: x: 2, y: 2, z: 4, core: 2. Of those that a mesh axis runs over, the one named last changes fastest.
Arguments:
- embeddings: bfloat16 [16384, 1024], P(('groups', 'rows', 'cols')), parts along dimension 0
- pair_list: int32 [16, 63, 2], P(('rows', 'cols')), may hold values from 0 to 31, as said below
- pair_count: int32 [16], P(('rows', 'cols')), may hold values from 1 to 63, as said below
Outputs:
- best_match: float32 [16384], P(('groups', 'rows', 'cols')), parts along dimension 0
There are 2 independent parts, one for each index of `groups`. A program takes and returns all parts, laid end to end along the dimension named above; an argument that names none is the same for every part. Nothing has to cross between parts.
Inputs may be any that keep to these rules, and one draw needn't show every extreme that they name: `pair_list`: device d = r * (devices along cols) + c lists pairs (a, b) with a among blocks r * 4 to r * 4 + 3 and b a block held by a device of cols index c, where device e holds blocks e * 2 to e * 2 + 1. Every pair of blocks a <= b appears exactly once over all devices, as (a, b) or (b, a). Entries past a device's count are zero. `pair_count`: some device holds exactly 63 pairs.
All inputs are finite; a program needn't handle non-finite values.
Results may differ from a plain program's by a relative error of at most 0.00051.
Values may be sent and summed in bfloat16 or wider, within the bound.
A program may use at most 128 MiB of HBM per device.

v0:
```python
import jax
import jax.numpy as jnp
from jax import lax
from jax.sharding import PartitionSpec as P

BLK = 256


lowest = -3.0
epsilon = 1e-06
pair_batch = 8


def shards(embeddings, pair_list, pair_count):
    row_devs = lax.axis_size("rows")
    col_devs = lax.axis_size("cols")
    band_index = lax.axis_index("rows")
    column_index = lax.axis_index("cols")
    local_rows = embeddings.shape[0]
    feature_len = embeddings.shape[1]
    blk_dev = local_rows // BLK
    band_blocks = blk_dev * col_devs
    col_blocks = blk_dev * row_devs
    values = embeddings.astype(jnp.float32)
    unit_rows = (
        values
        * lax.rsqrt(jnp.mean(values * values, axis=1, keepdims=True) + epsilon)
        * feature_len ** (-0.5)
    ).astype(jnp.bfloat16)
    band_data = lax.all_gather(unit_rows, "cols", axis=0, tiled=True)
    pair_rows = pair_list[0]
    live_count = pair_count[0]
    band_first = band_index * band_blocks
    row_local = pair_rows[:, 0] - band_first
    owner_dev = pair_rows[:, 1] // blk_dev
    col_local = owner_dev // col_devs * blk_dev + pair_rows[:, 1] % blk_dev
    band_ids = jnp.arange(band_blocks, dtype=jnp.int32)
    column_ids = jnp.arange(col_blocks, dtype=jnp.int32)
    column_data = lax.all_gather(unit_rows, "rows", axis=0, tiled=True)
    band_three = band_data.reshape(band_blocks, BLK, feature_len)
    column_three = column_data.reshape(col_blocks, BLK, feature_len)
    diagonal = jnp.eye(BLK, dtype=bool)
    group_turns = (live_count + pair_batch - 1) // pair_batch

    def visit(turn, state):
        row_best, col_best = state
        slot_ids = turn * pair_batch + jnp.arange(pair_batch, dtype=jnp.int32)
        live_slots = slot_ids < live_count
        row_slot = jnp.take(row_local, slot_ids, mode="clip")
        col_slot = jnp.take(col_local, slot_ids, mode="clip")
        same_block = jnp.take(pair_rows[:, 0], slot_ids, mode="clip") == jnp.take(
            pair_rows[:, 1], slot_ids, mode="clip"
        )
        left_blocks = jnp.take(band_three, row_slot, axis=0)
        right_blocks = jnp.take(column_three, col_slot, axis=0)
        similar = jnp.einsum(
            "pid,pjd->pij", left_blocks, right_blocks, preferred_element_type=jnp.float32
        )
        masked = (
            same_block[:, None, None] & diagonal[None] | jnp.logical_not(live_slots)[:, None, None]
        )
        similar = jnp.where(masked, lowest, similar)
        row_part = jnp.max(similar, axis=2)
        col_part = jnp.max(similar, axis=1)
        row_spread = jnp.where(
            row_slot[:, None, None] == band_ids[None, :, None], row_part[:, None, :], lowest
        )
        col_spread = jnp.where(
            col_slot[:, None, None] == column_ids[None, :, None], col_part[:, None, :], lowest
        )
        row_best = jnp.maximum(row_best, jnp.max(row_spread, axis=0))
        col_best = jnp.maximum(col_best, jnp.max(col_spread, axis=0))
        return (row_best, col_best)

    start_state = (
        jnp.full((band_blocks, BLK), lowest, jnp.float32),
        jnp.full((col_blocks, BLK), lowest, jnp.float32),
    )
    row_best, col_best = lax.fori_loop(0, group_turns, visit, start_state)
    band_all = lax.pmax(row_best, "cols")
    own_band = lax.dynamic_slice_in_dim(band_all, column_index * blk_dev, blk_dev, 0)
    column_all = lax.pmax(col_best, "rows")
    own_column = lax.dynamic_slice_in_dim(column_all, band_index * blk_dev, blk_dev, 0)
    return jnp.maximum(own_band, own_column).reshape(blk_dev * BLK)


def solution(mesh):
    in_specs = (
        P(("groups", "rows", "cols"), None),
        P(("rows", "cols"), None, None),
        P(("rows", "cols")),
    )
    out_specs = P(("groups", "rows", "cols"))
    return jax.shard_map(shards, mesh=mesh, in_specs=in_specs, out_specs=out_specs, check_vma=False)
```

profile of v0, /device:TPU:0, one launch (start us, length us, event | category | flops | bytes accessed | tf_op | source)
XLA Modules:
  0.0 330.5 jit_solution(1819935698627546649)
XLA Ops:
  6.5 1.5 fusion.17
  8.1 2.6 fusion.19
  10.7 0.7 all-gather.5.cloned.1.call-update
  12.2 12.0 %all-gather.3.cloned.1.call-done = bf16[1024,1024]{1,0:T(8,128)(2,1)} async-done(((bf16[512,1024]{1,0:T(8,128)(2,1)}), bf16[1024,1024]{1,0:T(8,128)(2,1)}) %all-gather.3.cloned.1.call-update) | async-done | bytes 2097168 | tf_op jit(solution)/shard_map/all_gather | solution.py:30
  24.1 128.3 %all-gather.5.cloned.1.call-done = bf16[4096,1024]{1,0:T(8,128)(2,1)} async-done(((bf16[512,1024]{1,0:T(8,128)(2,1)}), bf16[4096,1024]{1,0:T(8,128)(2,1)}) %all-gather.5.cloned.1.call-update) | async-done | bytes 8388624 | tf_op jit(solution)/shard_map/all_gather | solution.py:39
  152.4 107.9 %while.13 = (s32[]{:T(128)}, f32[4,256]{1,0:T(4,128)S(1)}, f32[16,256]{1,0:T(8,128)S(1)}, s32[]{:T(128)}, s32[63]{0:T(128)S(1)}, /*index=5*/s32[63,2]{0,1:T(2,12...) while((s32[]{:T(128)}, f32[4,256]{1,0:T(4,128)S(1)}, ...), condition=%wide.region_6.7_spmd.clone, body=%wide.region_1.6_spmd.clone.sunk | while | flops 1080704256 | bytes 33814936 | solution.py:79
  153.1 0.6 gather_fusion.4
  153.7 0.6 gather_fusion
  154.4 0.6 gather_fusion.1
  155.1 6.3 %gather_fusion.3 = bf16[8,256,1024]{2,1,0:T(8,128)(2,1)} fusion(bf16[16,256,1024]{2,1,0:T(8,128)(2,1)} %get-tuple-element.234, s32[1024]{0:T(1024)S(1)} %pad_clamp_fusion.7), kind=kCustom, calls=%fused_computation.5.clone.clone.1 | custom fusion | bytes 8388640 | tf_op jit(solution)/shard_map/while/body/jit(_take)/gather | solution.py:55
  161.4 2.8 gather_fusion.5
  164.2 0.7 compare_not_fusion.2
  164.9 5.2 %fusion.26 = (f32[8,256]{1,0:T(8,128)S(1)}, f32[8,256]{1,0:T(8,128)S(1)}) fusion(pred[8]{0:T(512)(128)(4,1)S(1)} %compare_not_fusion.2, pred[256,256]{1,0:T(8,128)(4,1)S(1)} %iota_compare_fusion.6, pred[8]{0:T(512)(128)(4,1)S(1)} %eq.76, bf16[8,256,1024]{2,1,0:T(8,128)(2,1)} %gather_fusion.3, pred[8]{0:T(512)(128)(4,1)S(1)} %get-tuple-element.197, ...), kind=kOutput, calls=%fused_computation.16.clone.1 | convolution fusion | flops 1080553472 | bytes 8470560 | tf_op jit(solution)/shard_map/while/body/pid,pjd->pij/dot_general | solution.py:56
  171.0 0.6 gather_fusion.4
  171.7 0.6 gather_fusion
  172.4 0.6 gather_fusion.1
  173.1 6.3 %gather_fusion.3 = bf16[8,256,1024]{2,1,0:T(8,128)(2,1)} fusion(bf16[16,256,1024]{2,1,0:T(8,128)(2,1)} %get-tuple-element.234, s32[1024]{0:T(1024)S(1)} %pad_clamp_fusion.7), kind=kCustom, calls=%fused_computation.5.clone.clone.1 | custom fusion | bytes 8388640 | tf_op jit(solution)/shard_map/while/body/jit(_take)/gather | solution.py:55
  179.4 2.8 gather_fusion.5
  182.2 0.7 compare_not_fusion.2
  182.9 5.2 %fusion.26 = (f32[8,256]{1,0:T(8,128)S(1)}, f32[8,256]{1,0:T(8,128)S(1)}) fusion(pred[8]{0:T(512)(128)(4,1)S(1)} %compare_not_fusion.2, pred[256,256]{1,0:T(8,128)(4,1)S(1)} %iota_compare_fusion.6, pred[8]{0:T(512)(128)(4,1)S(1)} %eq.76, bf16[8,256,1024]{2,1,0:T(8,128)(2,1)} %gather_fusion.3, pred[8]{0:T(512)(128)(4,1)S(1)} %get-tuple-element.197, ...), kind=kOutput, calls=%fused_computation.16.clone.1 | convolution fusion | flops 1080553472 | bytes 8470560 | tf_op jit(solution)/shard_map/while/body/pid,pjd->pij/dot_general | solution.py:56
  189.0 0.6 gather_fusion.4
  189.7 0.6 gather_fusion
  190.3 0.6 gather_fusion.1
  191.0 6.3 %gather_fusion.3 = bf16[8,256,1024]{2,1,0:T(8,128)(2,1)} fusion(bf16[16,256,1024]{2,1,0:T(8,128)(2,1)} %get-tuple-element.234, s32[1024]{0:T(1024)S(1)} %pad_clamp_fusion.7), kind=kCustom, calls=%fused_computation.5.clone.clone.1 | custom fusion | bytes 8388640 | tf_op jit(solution)/shard_map/while/body/jit(_take)/gather | solution.py:55
  197.4 2.8 gather_fusion.5
  200.2 0.7 compare_not_fusion.2
  200.8 5.2 %fusion.26 = (f32[8,256]{1,0:T(8,128)S(1)}, f32[8,256]{1,0:T(8,128)S(1)}) fusion(pred[8]{0:T(512)(128)(4,1)S(1)} %compare_not_fusion.2, pred[256,256]{1,0:T(8,128)(4,1)S(1)} %iota_compare_fusion.6, pred[8]{0:T(512)(128)(4,1)S(1)} %eq.76, bf16[8,256,1024]{2,1,0:T(8,128)(2,1)} %gather_fusion.3, pred[8]{0:T(512)(128)(4,1)S(1)} %get-tuple-element.197, ...), kind=kOutput, calls=%fused_computation.16.clone.1 | convolution fusion | flops 1080553472 | bytes 8470560 | tf_op jit(solution)/shard_map/while/body/pid,pjd->pij/dot_general | solution.py:56
  206.4 0.6 gather_fusion.2
  207.0 0.6 gather_fusion.4
  208.3 0.6 gather_fusion.1
  209.0 6.3 %gather_fusion.3 = bf16[8,256,1024]{2,1,0:T(8,128)(2,1)} fusion(bf16[16,256,1024]{2,1,0:T(8,128)(2,1)} %get-tuple-element.234, s32[1024]{0:T(1024)S(1)} %pad_clamp_fusion.7), kind=kCustom, calls=%fused_computation.5.clone.clone.1 | custom fusion | bytes 8388640 | tf_op jit(solution)/shard_map/while/body/jit(_take)/gather | solution.py:55
  215.4 2.8 gather_fusion.5
  218.1 0.7 compare_not_fusion.2
  218.8 5.2 %fusion.26 = (f32[8,256]{1,0:T(8,128)S(1)}, f32[8,256]{1,0:T(8,128)S(1)}) fusion(pred[8]{0:T(512)(128)(4,1)S(1)} %compare_not_fusion.2, pred[256,256]{1,0:T(8,128)(4,1)S(1)} %iota_compare_fusion.6, pred[8]{0:T(512)(128)(4,1)S(1)} %eq.76, bf16[8,256,1024]{2,1,0:T(8,128)(2,1)} %gather_fusion.3, pred[8]{0:T(512)(128)(4,1)S(1)} %get-tuple-element.197, ...), kind=kOutput, calls=%fused_computation.16.clone.1 | convolution fusion | flops 1080553472 | bytes 8470560 | tf_op jit(solution)/shard_map/while/body/pid,pjd->pij/dot_general | solution.py:56
  225.0 0.6 gather_fusion.4
  226.3 0.6 gather_fusion.1
  227.0 6.3 %gather_fusion.3 = bf16[8,256,1024]{2,1,0:T(8,128)(2,1)} fusion(bf16[16,256,1024]{2,1,0:T(8,128)(2,1)} %get-tuple-element.234, s32[1024]{0:T(1024)S(1)} %pad_clamp_fusion.7), kind=kCustom, calls=%fused_computation.5.clone.clone.1 | custom fusion | bytes 8388640 | tf_op jit(solution)/shard_map/while/body/jit(_take)/gather | solution.py:55
  233.3 2.8 gather_fusion.5
  236.1 0.7 compare_not_fusion.2
  236.8 5.2 %fusion.26 = (f32[8,256]{1,0:T(8,128)S(1)}, f32[8,256]{1,0:T(8,128)S(1)}) fusion(pred[8]{0:T(512)(128)(4,1)S(1)} %compare_not_fusion.2, pred[256,256]{1,0:T(8,128)(4,1)S(1)} %iota_compare_fusion.6, pred[8]{0:T(512)(128)(4,1)S(1)} %eq.76, bf16[8,256,1024]{2,1,0:T(8,128)(2,1)} %gather_fusion.3, pred[8]{0:T(512)(128)(4,1)S(1)} %get-tuple-element.197, ...), kind=kOutput, calls=%fused_computation.16.clone.1 | convolution fusion | flops 1080553472 | bytes 8470560 | tf_op jit(solution)/shard_map/while/body/pid,pjd->pij/dot_general | solution.py:56
  243.0 0.6 gather_fusion.4
  244.3 0.6 gather_fusion.1
  245.0 6.3 %gather_fusion.3 = bf16[8,256,1024]{2,1,0:T(8,128)(2,1)} fusion(bf16[16,256,1024]{2,1,0:T(8,128)(2,1)} %get-tuple-element.234, s32[1024]{0:T(1024)S(1)} %pad_clamp_fusion.7), kind=kCustom, calls=%fused_computation.5.clone.clone.1 | custom fusion | bytes 8388640 | tf_op jit(solution)/shard_map/while/body/jit(_take)/gather | solution.py:55
  251.3 2.8 gather_fusion.5
  254.1 0.7 compare_not_fusion.2
  254.8 5.2 %fusion.26 = (f32[8,256]{1,0:T(8,128)S(1)}, f32[8,256]{1,0:T(8,128)S(1)}) fusion(pred[8]{0:T(512)(128)(4,1)S(1)} %compare_not_fusion.2, pred[256,256]{1,0:T(8,128)(4,1)S(1)} %iota_compare_fusion.6, pred[8]{0:T(512)(128)(4,1)S(1)} %eq.76, bf16[8,256,1024]{2,1,0:T(8,128)(2,1)} %gather_fusion.3, pred[8]{0:T(512)(128)(4,1)S(1)} %get-tuple-element.197, ...), kind=kOutput, calls=%fused_computation.16.clone.1 | convolution fusion | flops 1080553472 | bytes 8470560 | tf_op jit(solution)/shard_map/while/body/pid,pjd->pij/dot_general | solution.py:56
  260.3 33.0 %pmax.15 = f32[16,256]{1,0:T(8,128)S(1)} all-reduce(f32[16,256]{1,0:T(8,128)S(1)} %get-tuple-element.75), channel_id=1, replica_groups=mesh['groups'=2,'rows'=8,'cols'=2] {'rows'}, use_global_device_ids=true, to_apply=%region_8.9 | all-reduce | flops 4096 | bytes 32768 | tf_op jit(solution)/shard_map/pmax | solution.py:82
  293.2 29.8 %pmax.14 = f32[4,256]{1,0:T(4,128)S(1)} all-reduce(f32[4,256]{1,0:T(4,128)S(1)} %get-tuple-element.74), channel_id=1, replica_groups=mesh['groups'=2,'rows'=8,'cols'=2] {'cols'}, use_global_device_ids=true, to_apply=%region_7.8 | all-reduce | flops 1024 | bytes 8192 | tf_op jit(solution)/shard_map/pmax | solution.py:80
  (128 shorter events, 8.0 us)
Async XLA Ops:
  6.5 5.6 %copy-start.1 = (s32[1,63,2]{1,2,0:T(2,128)S(1)}, s32[1,63,2]{1,2,0:T(2,128)}, u32[]{:S(2)}) copy-start(s32[1,63,2]{1,2,0:T(2,128)} %param.6) | copy-start | bytes 1516
  6.5 17.6 %all-gather.3.cloned.1.call-start = ((), (), s32[]{:S(2)}) async-start(), calls=%async_computation | async-start | bytes 3145728 | tf_op jit(solution)/shard_map/all_gather | solution.py:30
  10.7 141.7 %all-gather.5.cloned.1.call-start = ((), (), s32[]{:S(2)}) async-start(), calls=%async_computation.1 | async-start | bytes 9437184 | tf_op jit(solution)/shard_map/all_gather | solution.py:39
  155.1 6.3 %copy-start = (bf16[4,256,1024]{2,1,0:T(8,128)(2,1)S(1)}, bf16[4,256,1024]{2,1,0:T(8,128)(2,1)}, u32[]{:S(2)}) copy-start(bf16[4,256,1024]{2,1,0:T(8,128)(2,1)} %get-tuple-element.232) | copy-start | bytes 6291460 | tf_op jit(solution)/shard_map/while
  173.1 6.3 %copy-start = (bf16[4,256,1024]{2,1,0:T(8,128)(2,1)S(1)}, bf16[4,256,1024]{2,1,0:T(8,128)(2,1)}, u32[]{:S(2)}) copy-start(bf16[4,256,1024]{2,1,0:T(8,128)(2,1)} %get-tuple-element.232) | copy-start | bytes 6291460 | tf_op jit(solution)/shard_map/while
  191.0 6.3 %copy-start = (bf16[4,256,1024]{2,1,0:T(8,128)(2,1)S(1)}, bf16[4,256,1024]{2,1,0:T(8,128)(2,1)}, u32[]{:S(2)}) copy-start(bf16[4,256,1024]{2,1,0:T(8,128)(2,1)} %get-tuple-element.232) | copy-start | bytes 6291460 | tf_op jit(solution)/shard_map/while
  209.0 6.3 %copy-start = (bf16[4,256,1024]{2,1,0:T(8,128)(2,1)S(1)}, bf16[4,256,1024]{2,1,0:T(8,128)(2,1)}, u32[]{:S(2)}) copy-start(bf16[4,256,1024]{2,1,0:T(8,128)(2,1)} %get-tuple-element.232) | copy-start | bytes 6291460 | tf_op jit(solution)/shard_map/while
  227.0 6.3 %copy-start = (bf16[4,256,1024]{2,1,0:T(8,128)(2,1)S(1)}, bf16[4,256,1024]{2,1,0:T(8,128)(2,1)}, u32[]{:S(2)}) copy-start(bf16[4,256,1024]{2,1,0:T(8,128)(2,1)} %get-tuple-element.232) | copy-start | bytes 6291460 | tf_op jit(solution)/shard_map/while
  245.0 6.3 %copy-start = (bf16[4,256,1024]{2,1,0:T(8,128)(2,1)S(1)}, bf16[4,256,1024]{2,1,0:T(8,128)(2,1)}, u32[]{:S(2)}) copy-start(bf16[4,256,1024]{2,1,0:T(8,128)(2,1)} %get-tuple-element.232) | copy-start | bytes 6291460 | tf_op jit(solution)/shard_map/while
Sparse Core Ops, SparseCore 0:
  10.8 13.2 all-gather.2
  26.2 126.0 all-gather.4
where the time goes:
time: 329 us; the launch traced here: 331 us
  waiting for transfers between devices  141 us (43%)
  local copies, waits for them, and re-layouts  70.7 us (21%)
  blocking collectives  62.8 us (19%)
  matrix products  31 us (9%)
  between operations  14.1 us (4%)
  other arithmetic  10.2 us (3%)
    all_gather x1, waiting for transfers between devices, shards(): column_data = lax.all_gather(unit_rows, 'rows', axis=0, tiled=True)  128 us
    gather x6, local copies, waits for them, and re-layouts, visit(): right_blocks = jnp.take(column_three, col_slot, axis=0)  37.9 us
    pmax x1, blocking collectives, shards(): column_all = lax.pmax(col_best, 'rows')  33 us
    dot_general x6, matrix products, visit(): jnp.einsum('pid,pjd->pij', left_blocks, right_blocks, preferred_element_t...  31 us
    pmax x1, blocking collectives, shards(): band_all = lax.pmax(row_best, 'cols')  29.8 us
    gather x6, local copies, waits for them, and re-layouts, visit(): left_blocks = jnp.take(band_three, row_slot, axis=0)  16.6 us
    all_gather x1, waiting for transfers between devices, shards(): band_data = lax.all_gather(unit_rows, 'cols', axis=0, tiled=True)  12 us
  transfers between devices with their start and end apart: 2, of which 2 were waited for; matrix products, arithmetic and copies ran while one was open for 0% of the time, Pallas kernels for 0%

commit v1 on v0

v1 whole, which is shorter than its diff:
```python
import functools
import itertools

import jax
import jax.numpy as jnp
from jax import lax
from jax.experimental import pallas as pl
from jax.experimental.pallas import tpu as pltpu
from jax.sharding import PartitionSpec as P

MESH = pl.DeviceIdType.MESH
BLK = 256
LANES = 128
SUBLANES = 8
lowest = -3.0
epsilon = 1e-06


class Plan:
    def __init__(self, chips):
        self.chips = chips
        if chips == 8:
            self.parts, self.steps = 1, 2
            self.moves = [
                [i ^ 1 for i in range(8)],
                [i + 2 if i < 6 else -1 for i in range(8)],
                [i - 2 if i > 1 else -1 for i in range(8)],
            ]
            second = [
                [2, 3, 4, 5, 2, 3, 4, 5],
                [1, 0, 3, 2, 2, 3, -1, -1],
                [-1, -1, 4, 5, 6, 7, 7, 6],
            ]
            self.sends = [
                [[(i, 0) if to[i] >= 0 else None for i in range(8)], [(u, 0) if u >= 0 else None for u in later]]
                for to, later in zip(self.moves, second)
            ]
        else:
            self.parts, self.steps = 1, chips // 2
            self.moves = [[(i + 1) % chips for i in range(chips)]]
            self.sends = [[[((i - t) % chips, 0) for i in range(chips)] for t in range(self.steps)]]
        self.slots = self.parts + len(self.moves) * self.steps
        self.unit_of = [[None] * self.slots for _ in range(chips)]
        self.held = [{} for _ in range(chips)]
        for i in range(chips):
            for h in range(self.parts):
                self.unit_of[i][h] = (i, h)
                self.held[i][(i, h)] = (0, h)
        self.source = [[[-1] * chips for _ in range(self.steps)] for _ in self.moves]
        for t in range(self.steps):
            arrived = []
            for d, to in enumerate(self.moves):
                for i in range(chips):
                    unit = self.sends[d][t][i]
                    if unit is None:
                        continue
                    self.source[d][t][i] = self.held[i][unit][1]
                    slot = self.parts + d * self.steps + t
                    self.unit_of[to[i]][slot] = unit
                    arrived.append((to[i], unit, slot))
            for i, unit, slot in arrived:
                self.held[i].setdefault(unit, (t + 1, slot))
        self.assign()

    def assign(self):
        units = [(i, h) for i in range(self.chips) for h in range(self.parts)]
        options = []
        for a, b in itertools.combinations_with_replacement(units, 2):
            places = []
            for i in range(self.chips):
                if a in self.held[i] and b in self.held[i]:
                    places.append((max(self.held[i][a][0], self.held[i][b][0]), i))
            assert places
            first = min(places)[0]
            places = [i for stage, i in places if stage == first]
            options.append((len(places), first, a, b, places))
        options.sort()
        load = [[0] * self.chips for _ in range(self.steps + 1)]
        chosen = []
        for _, stage, a, b, places in options:
            i = min(places, key=lambda k: (load[stage][k], k))
            load[stage][i] += 1
            chosen.append([stage, a, b, places, i])
        moved = True
        while moved:
            moved = False
            for item in chosen:
                stage, a, b, places, i = item
                for k in places:
                    if load[stage][k] + 1 < load[stage][i]:
                        load[stage][k] += 1
                        load[stage][i] -= 1
                        item[4] = i = k
                        moved = True
        self.work = [[[] for _ in range(self.chips)] for _ in range(self.steps + 1)]
        for stage, a, b, _, i in chosen:
            one, two = self.held[i][a], self.held[i][b]
            u, v = (one, two) if one[0] >= two[0] else (two, one)
            self.work[stage][i].append((u[1], v[1]))
        for stage in self.work:
            longest = max(len(pairs) for pairs in stage)
            for pairs in stage:
                while len(pairs) < longest:
                    pairs.append(pairs[-1] if pairs else (0, 0))


def pick(values, index):
    if all(v == values[0] for v in values):
        return jnp.int32(values[0])
    result = jnp.int32(values[-1])
    for i in range(len(values) - 1):
        result = jnp.where(index == i, jnp.int32(values[i]), result)
    return result


def kernel(
    plan, cols, x_ref, o_ref, buf, row_acc, col_acc, parts, got,
    send_sem, recv_sem, side_send, side_recv, part_send, part_recv,
):
    me, core = lax.axis_index("rows"), lax.axis_index("cols")
    chips, steps, own = plan.chips, plan.steps, plan.parts
    rows, width = x_ref.shape
    unit = rows // own
    others = [(k, q) for k in range(chips) for q in range(cols) if (k, q) != (0, 0)]

    def device(k, q):
        return {"rows": lax.rem(me + k, chips), "cols": lax.rem(core + q, cols)}

    barrier = pltpu.get_barrier_semaphore()
    for k, q in others:
        pl.semaphore_signal(barrier, inc=1, device_id=device(k, q), device_id_type=MESH)

    for h in range(own):
        values = x_ref[h * unit:(h + 1) * unit, :].astype(jnp.float32)
        mean = jnp.mean(values * values, axis=1, keepdims=True)
        buf[h, 0] = (values * lax.rsqrt(mean + epsilon) * width ** (-0.5)).astype(jnp.bfloat16)

    pl.semaphore_wait(barrier, len(others))

    def present(table, index):
        return pick([int(v >= 0) for v in table], index) == 1

    def guarded(table, index, action):
        if all(v >= 0 for v in table):
            action()
        elif any(v >= 0 for v in table):
            pl.when(present(table, index))(action)

    def link_copy(d, t):
        slot = own + d * steps + t
        return pltpu.make_async_remote_copy(
            src_ref=buf.at[pick([max(v, 0) for v in plan.source[d][t]], me), 0],
            dst_ref=buf.at[slot, 0],
            send_sem=send_sem.at[d, t],
            recv_sem=recv_sem.at[d, t],
            device_id={"rows": pick([max(v, 0) for v in plan.moves[d]], me), "cols": core},
            device_id_type=MESH,
        )

    def incoming(d, t):
        result = [-1] * chips
        for i in range(chips):
            if plan.source[d][t][i] >= 0:
                result[plan.moves[d][i]] = 1
        return result

    def side_copy(slot, q):
        return pltpu.make_async_remote_copy(
            src_ref=buf.at[slot, 0],
            dst_ref=buf.at[slot, (cols - q) % cols],
            send_sem=side_send.at[slot, q],
            recv_sem=side_recv.at[slot, (cols - q) % cols],
            device_id=device(0, q),
            device_id_type=MESH,
        )

    def start_sends(t):
        for d in range(len(plan.moves)):
            guarded(plan.source[d][t], me, lambda: link_copy(d, t).start())

    def tile(u, v, q, col0, same):
        left = buf[u, 0]
        right = buf[v, q, pl.ds(col0, BLK), :]
        similar = lax.dot_general(
            left, right, (((1,), (1,)), ((), ())), preferred_element_type=jnp.float32
        )
        row_ids = lax.broadcasted_iota(jnp.int32, similar.shape, 0)
        col_ids = lax.broadcasted_iota(jnp.int32, similar.shape, 1) + col0
        limit = jnp.where(same, 0, rows)
        similar = jnp.where(row_ids == col_ids + limit, lowest, similar)
        best = row_acc[u]
        for j in range(BLK // LANES):
            best = jnp.maximum(best, similar[:, j * LANES:(j + 1) * LANES])
        row_acc[u] = best
        tall = jnp.max(similar.reshape(unit // SUBLANES, SUBLANES, BLK), axis=0)
        col_acc[v, q, :, pl.ds(col0, BLK)] = jnp.maximum(col_acc[v, q, :, pl.ds(col0, BLK)], tall)

    def multiply(stage):
        lists = plan.work[stage]
        count = len(lists[0])
        if not count:
            return
        bits = max(plan.slots - 1, 1).bit_length()
        per_word = 30 // (2 * bits)
        words = []
        for first in range(0, count, per_word):
            packed = []
            for i in range(chips):
                word = 0
                for n, (u, v) in enumerate(lists[i][first:first + per_word]):
                    word |= (u | v << bits) << (2 * bits * n)
                packed.append(word)
            words.append(pick(packed, me))
        tiles = unit // BLK

        @pl.loop(0, count * cols * tiles)
        def _(step):
            p, rest = step // (cols * tiles), step % (cols * tiles)
            q, j = rest // tiles, rest % tiles
            word = words[0]
            for n in range(1, len(words)):
                word = jnp.where(p >= n * per_word, words[n], word)
            word = word >> (2 * bits * (p % per_word))
            u, v = word & (2 ** bits - 1), (word >> bits) & (2 ** bits - 1)
            tile(u, v, q, pl.multiple_of(j * BLK, BLK), (u == v) & (q == 0))

    start_sends(0)
    for h in range(own):
        for q in range(1, cols):
            side_copy(h, q).start()
    row_acc[...] = jnp.full(row_acc.shape, lowest, jnp.float32)
    col_acc[...] = jnp.full(col_acc.shape, lowest, jnp.float32)
    parts[...] = jnp.full(parts.shape, lowest, jnp.float32)
    for h in range(own):
        for q in range(1, cols):
            side_copy(h, q).wait_recv()
    multiply(0)
    for t in range(steps):
        for d in range(len(plan.moves)):
            guarded(incoming(d, t), me, lambda: link_copy(d, t).wait_recv())
        if t + 1 < steps:
            start_sends(t + 1)
        for d in range(len(plan.moves)):
            for q in range(1, cols):
                guarded(incoming(d, t), me, lambda: side_copy(own + d * steps + t, q).start())
        for d in range(len(plan.moves)):
            for q in range(1, cols):
                guarded(incoming(d, t), me, lambda: side_copy(own + d * steps + t, q).wait_recv())
        multiply(t + 1)

    for slot in range(plan.slots):
        names = [plan.unit_of[i][slot] for i in range(chips)]
        chip_table = [name[0] if name else -1 for name in names]
        part_table = [name[1] if name else 0 for name in names]

        def fold():
            chip, part = pick([max(v, 0) for v in chip_table], me), pick(part_table, me)
            across = jnp.max(jnp.transpose(row_acc[slot]), axis=0, keepdims=True)
            for q in range(cols):
                best = jnp.max(col_acc[slot, q], axis=0, keepdims=True)
                if q == 0:
                    best = jnp.maximum(best, across)
                place = chip * cols + q
                parts[place, part] = jnp.maximum(parts[place, part], best)

        guarded(chip_table, me, fold)

    def part_copy(k, q):
        return pltpu.make_async_remote_copy(
            src_ref=parts.at[lax.rem(me + k, chips) * cols + q],
            dst_ref=got.at[k * cols + q],
            send_sem=part_send.at[k * cols + q],
            recv_sem=part_recv.at[k * cols + q],
            device_id=device(k, q),
            device_id_type=MESH,
        )

    for k, q in others:
        part_copy(k, q).start()
    result = parts[me * cols]
    for k, q in others:
        part_copy(k, q).wait_recv()
    for k, q in others:
        result = jnp.maximum(result, got[k * cols + q])
    for h in range(own):
        o_ref[:, h * unit:(h + 1) * unit] = result[h]

    for k, q in others:
        part_copy(k, q).wait_send()
    for t in range(steps):
        for d in range(len(plan.moves)):
            guarded(plan.source[d][t], me, lambda: link_copy(d, t).wait_send())
            for q in range(1, cols):
                guarded(incoming(d, t), me, lambda: side_copy(own + d * steps + t, q).wait_send())
    for h in range(own):
        for q in range(1, cols):
            side_copy(h, q).wait_send()


def shards(embeddings, pair_list, pair_count):
    chips, cols = lax.axis_size("rows"), lax.axis_size("cols")
    rows, width = embeddings.shape
    plan = Plan(chips)
    unit = rows // plan.parts
    total = chips * cols
    best = pl.pallas_call(
        functools.partial(kernel, plan, cols),
        out_shape=jax.ShapeDtypeStruct((1, rows), jnp.float32),
        in_specs=[pl.BlockSpec(memory_space=pltpu.VMEM)],
        out_specs=pl.BlockSpec(memory_space=pltpu.VMEM),
        scratch_shapes=[
            pltpu.VMEM((plan.slots, cols, unit, width), jnp.bfloat16),
            pltpu.VMEM((plan.slots, unit, LANES), jnp.float32),
            pltpu.VMEM((plan.slots, cols, SUBLANES, unit), jnp.float32),
            pltpu.VMEM((total, plan.parts, 1, unit), jnp.float32),
            pltpu.VMEM((total, plan.parts, 1, unit), jnp.float32),
            pltpu.SemaphoreType.DMA((len(plan.moves), plan.steps)),
            pltpu.SemaphoreType.DMA((len(plan.moves), plan.steps)),
            pltpu.SemaphoreType.DMA((plan.slots, cols)),
            pltpu.SemaphoreType.DMA((plan.slots, cols)),
            pltpu.SemaphoreType.DMA((total,)),
            pltpu.SemaphoreType.DMA((total,)),
        ],
        compiler_params=pltpu.CompilerParams(
            collective_id=0, has_side_effects=True, vmem_limit_bytes=48 * 2 ** 20
        ),
    )(embeddings)
    return best.reshape(rows)


def solution(mesh):
    in_specs = (
        P(("groups", "rows", "cols"), None),
        P(("rows", "cols"), None, None),
        P(("rows", "cols")),
    )
    out_specs = P(("groups", "rows", "cols"))
    return jax.shard_map(shards, mesh=mesh, in_specs=in_specs, out_specs=out_specs, check_vma=False)
```

time: 329 us -> 69.9 us (0.21)
  waiting for transfers between devices: 141 us -> 0 us
  local copies, waits for them, and re-layouts: 70.7 us -> 1.8 us
  Pallas kernels: 0 us -> 68 us
  blocking collectives: 62.8 us -> 0 us
  matrix products: 31 us -> 0 us
  between operations: 14.1 us -> 0.01 us
  other arithmetic: 10.2 us -> 0 us
    all_gather x2 -> x0, waiting for transfers between devices: 140 us -> none  [the longest x1 128 us: shards(): column_data = lax.all_gather(unit_rows, 'rows', axis=0, tiled=True)]
    gather x36 -> x0, local copies, waits for them, and re-layouts: 70.1 us -> none  [the longest x6 37.9 us: visit(): right_blocks = jnp.take(column_three, col_slot, axis=0)]
    pallas_call x0 -> x1, Pallas kernels: none -> 68 us  [shards(): pl.pallas_call(functools.partial(kernel, plan, cols), out_shape=jax.Shape...]
    pmax x2 -> x0, blocking collectives: 62.8 us -> none  [the longest x1 33 us: shards(): column_all = lax.pmax(col_best, 'rows')]
    dot_general x6 -> x0, matrix products: 31 us -> none  [visit(): jnp.einsum('pid,pjd->pij', left_blocks, right_blocks, preferred_element_t...]
    not x6 -> x0, other arithmetic: 3.91 us -> none  [visit(): jnp.logical_not(live_slots)[:, None, None]]
  transfers between devices with their start and end apart: 2 -> 0, of which waited for: 2 -> 0; matrix products, arithmetic and copies ran while one was open for 0% -> 0% of each run, Pallas kernels for 0% -> 0%
where the time goes in v1:
time: 69.9 us; the launch traced here: 69.8 us
  Pallas kernels  68 us (97%)
  local copies, waits for them, and re-layouts  1.8 us (3%)
    pallas_call x1, Pallas kernels, shards(): pl.pallas_call(functools.partial(kernel, plan, cols), out_shape=jax.Shape...  68 us
    unnamed x3, local copies, waits for them, and re-layouts  1.8 us

profile of v1, /device:TPU:0, one launch (start us, length us, event | category | flops | bytes accessed | tf_op | source)
XLA Modules:
  0.0 69.8 jit_solution(12726420688098750674)
XLA Ops:
  0.0 0.0 copy-start
  0.0 1.2 %copy-done = bf16[512,1024]{1,0:T(8,128)(2,1)S(1)} copy-done((bf16[512,1024]{1,0:T(8,128)(2,1)S(1)}, bf16[512,1024]{1,0:T(8,128)(2,1)}, u32[]{:S(2)}) %copy-start) | copy-done | bytes 1048600
  1.2 68.0 %shard_map.17 = f32[1,512]{1,0:T(1,128)S(1)} custom-call(bf16[512,1024]{1,0:T(8,128)(2,1)S(1)} %copy-done), custom_call_target="tpu_custom_call" | custom-call | tf_op jit(solution)/shard_map/pallas_call | solution.py:306
  69.2 0.6 copy.3
Async XLA Ops:
  0.0 1.2 %copy-start = (bf16[512,1024]{1,0:T(8,128)(2,1)S(1)}, bf16[512,1024]{1,0:T(8,128)(2,1)}, u32[]{:S(2)}) copy-start(bf16[512,1024]{1,0:T(8,128)(2,1)} %x_ref.1) | copy-start | bytes 3145732

commit v2 on v1

--- a/solution.py
+++ b/solution.py
@@ -19,26 +19,9 @@
 class Plan:
     def __init__(self, chips):
         self.chips = chips
-        if chips == 8:
-            self.parts, self.steps = 1, 2
-            self.moves = [
-                [i ^ 1 for i in range(8)],
-                [i + 2 if i < 6 else -1 for i in range(8)],
-                [i - 2 if i > 1 else -1 for i in range(8)],
-            ]
-            second = [
-                [2, 3, 4, 5, 2, 3, 4, 5],
-                [1, 0, 3, 2, 2, 3, -1, -1],
-                [-1, -1, 4, 5, 6, 7, 7, 6],
-            ]
-            self.sends = [
-                [[(i, 0) if to[i] >= 0 else None for i in range(8)], [(u, 0) if u >= 0 else None for u in later]]
-                for to, later in zip(self.moves, second)
-            ]
-        else:
-            self.parts, self.steps = 1, chips // 2
-            self.moves = [[(i + 1) % chips for i in range(chips)]]
-            self.sends = [[[((i - t) % chips, 0) for i in range(chips)] for t in range(self.steps)]]
+        self.parts, self.steps = 1, chips // 2
+        self.moves = [[(i + 1) % chips for i in range(chips)]]
+        self.sends = [[[((i - t) % chips, 0) for i in range(chips)] for t in range(self.steps)]]
         self.slots = self.parts + len(self.moves) * self.steps
         self.unit_of = [[None] * self.slots for _ in range(chips)]
         self.held = [{} for _ in range(chips)]
@@ -297,9 +280,337 @@
             side_copy(h, q).wait_send()
 
 
+OWN, YNB, LOW, FAR, TOP, PASS, BACK = range(7)
+CHUNKS = 8
+PIECE = 128
+ALL, FIRST, SECOND = range(CHUNKS), range(CHUNKS // 2), range(CHUNKS // 2, CHUNKS)
+A_ORDER = list(SECOND) + list(FIRST)
+ROUTES = {
+    (0, OWN): [("x", PASS, A_ORDER), ("u", LOW, ALL), ("y", YNB, ALL)],
+    (1, OWN): [("u", LOW, ALL), ("y", YNB, ALL)],
+    (2, OWN): [("y", YNB, ALL)],
+    (3, OWN): [("x", BACK, SECOND), ("d", TOP, FIRST), ("y", YNB, ALL)],
+    (3, PASS): [("d", PASS, ALL)],
+    (2, PASS): [("d", PASS, ALL)],
+    (1, PASS): [("x", FAR, ALL), ("d", PASS, SECOND)],
+    (0, PASS): [("x", FAR, SECOND)],
+    (0, BACK): [("u", BACK, SECOND)],
+    (1, BACK): [("x", TOP, SECOND)],
+    (2, LOW): [("u", LOW, ALL)],
+    (2, FAR): [("u", FAR, FIRST)],
+}
+OWNER = {OWN: [0, 1, 2, 3], YNB: [0, 1, 2, 3], LOW: [-1, 0, 1, 1], FAR: [-1, -1, 0, 0], TOP: [-1, -1, 3, -1]}
+BUDGET = 6
+
+
+def target(place, way):
+    return {"x": 3 - place, "y": place, "u": place + 1, "d": place - 1}[way]
+
+
+def relay_plan():
+    def depth(place, slot, chunk):
+        return max(
+            [1 + depth(target(place, way), to, chunk) for way, to, which in ROUTES.get((place, slot), []) if chunk in which],
+            default=0,
+        )
+
+    queues = {}
+
+    def enqueue(place, slot, chunk, step, order):
+        for way, to, which in ROUTES.get((place, slot), []):
+            if chunk in which:
+                rank = -1 - depth(target(place, way), to, chunk)
+                place_in = list(which).index(chunk) if slot == OWN else order
+                queues.setdefault((place, way), []).append((rank, place_in, slot, to, chunk, step))
+
+    arrived = {(p, OWN, c): 0 for p in range(4) for c in ALL}
+    for p in range(4):
+        for c in ALL:
+            enqueue(p, OWN, c, 0, c)
+    waits, sends, step = [], [], 0
+    landing = []
+    while landing or any(queues.values()):
+        waits.append([[] for _ in range(4)])
+        sends.append([[] for _ in range(4)])
+        for p, slot, c in landing:
+            arrived[p, slot, c] = step
+            waits[step][p].append((slot, c))
+            enqueue(p, slot, c, step, step)
+        landing = []
+        for (p, way), queue in queues.items():
+            if queue:
+                item = min(queue)
+                queue.remove(item)
+                _, _, slot, to, c, ready = item
+                sends[max(ready, step - 1)][p].append((way, slot, to, c))
+                landing.append((target(p, way), to, c))
+        step += 1
+    steps = len(waits)
+    share = max(arrived[p, YNB, c] for p in range(4) for c in ALL)
+    work = [[[] for _ in range(4)] for _ in range(steps + 1)]
+    for p in range(4):
+        jobs = []
+        pieces = range(2)
+
+        def ready(slot, piece):
+            per = CHUNKS // PIECES
+            return max(arrived[p, slot, c] for c in range(piece * per, piece * per + per))
+
+        for piece in range(PIECES):
+            jobs += [(1, (OWN, piece, OWN, q)) for q in range(2)]
+            jobs.append((share + 1, (OWN, piece, YNB, 2)))
+            for slot in (LOW, FAR, TOP):
+                if OWNER[slot][p] >= 0:
+                    at = ready(slot, piece)
+                    jobs += [(max(1, at), (slot, piece, OWN, q)) for q in range(2)]
+                    jobs += [(max(share + 1, at), (slot, piece, YNB, q)) for q in range(2)]
+        if p == 0:
+            jobs = [j for j in jobs]
+        jobs.sort()
+        for t in range(steps + 1):
+            able = [j for j in jobs if j[0] <= t]
+            take = able if t == steps else able[:BUDGET]
+            work[t][p] = [j[1] for j in take]
+            jobs = [j for j in jobs if j not in take]
+        assert not jobs
+    return waits, sends, work, share
+
+
+PIECES = 512 // PIECE
+
+
+def relay_kernel(
+    x_ref, o_ref, buf, row_acc, col_acc, parts, got,
+    send_sem, recv_sem, side_send, side_recv, part_send, part_recv,
+):
+    waits, sends, work, share = relay_plan()
+    group, line, core = lax.axis_index("groups"), lax.axis_index("rows"), lax.axis_index("cols")
+    z, y = line // 2, line % 2
+    place = z + group * (3 - 2 * z)
+    rows, width = x_ref.shape
+    chunk_rows = rows // CHUNKS
+    upward = 1 - 2 * group
+
+    def neighbour(way):
+        if way == "x":
+            return {"groups": 1 - group, "rows": line, "cols": core}
+        if way == "y":
+            return {"groups": group, "rows": 2 * z + 1 - y, "cols": core}
+        step = upward if way == "u" else -upward
+        return {"groups": group, "rows": line + 2 * step, "cols": core}
+
+    def device_at(at, dy, q):
+        zz = at + group * (3 - 2 * at)
+        return {"groups": group, "rows": 2 * zz + (y + dy) % 2, "cols": (core + q) % 2}
+
+    barrier = pltpu.get_barrier_semaphore()
+    everyone = [(k, q) for k in range(8) for q in range(2) if (k, q) != (0, 0)]
+    pl.semaphore_signal(barrier, inc=1, device_id=neighbour("x"), device_id_type=MESH)
+    for k, q in everyone:
+        other = {"groups": group, "rows": (line + k) % 8, "cols": (core + q) % 2}
+        pl.semaphore_signal(barrier, inc=1, device_id=other, device_id_type=MESH)
+
+    @pl.loop(0, CHUNKS)
+    def _(c):
+        at = pl.ds(pl.multiple_of(c * chunk_rows, chunk_rows), chunk_rows)
+        values = x_ref[at, :].astype(jnp.float32)
+        mean = jnp.mean(values * values, axis=1, keepdims=True)
+        buf[OWN, 0, at, :] = (values * lax.rsqrt(mean + epsilon) * width ** (-0.5)).astype(jnp.bfloat16)
+
+    pl.semaphore_wait(barrier, len(everyone) + 1)
+
+    def link_copy(way, slot, to, c, n):
+        at = pl.ds(c * chunk_rows, chunk_rows)
+        return pltpu.make_async_remote_copy(
+            src_ref=buf.at[slot, 0, at],
+            dst_ref=buf.at[to, 0, at],
+            send_sem=send_sem.at[n],
+            recv_sem=recv_sem.at[to, c],
+            device_id=neighbour(way),
+            device_id_type=MESH,
+        )
+
+    def arrival(slot, c):
+        return link_copy("x", slot, slot, c, 0)
+
+    def side_copy(n):
+        slot = OWN if n == 0 else YNB
+        return pltpu.make_async_remote_copy(
+            src_ref=buf.at[slot, 0],
+            dst_ref=buf.at[slot, 1],
+            send_sem=side_send.at[n],
+            recv_sem=side_recv.at[n],
+            device_id={"groups": group, "rows": line, "cols": 1 - core},
+            device_id_type=MESH,
+        )
+
+    def multiply(lists):
+        longest = max(len(items) for items in lists)
+        if not longest:
+            return
+        packed = [
+            [sum((u | piece << 3 | v << 6 | q << 7) << (9 * i) for i, (u, piece, v, q) in enumerate(items[n:n + 3]))
+             for items in lists]
+            for n in range(0, longest, 3)
+        ]
+        words = [pick(entry, place) for entry in packed]
+
+        @pl.loop(0, pick([len(items) for items in lists], place))
+        def _(n):
+            word = words[0]
+            for k in range(1, len(words)):
+                word = jnp.where(n >= 3 * k, words[k], word)
+            word = word >> (9 * (n % 3))
+            u, piece, v, q = word & 7, (word >> 3) & 7, (word >> 6) & 1, (word >> 7) & 3
+            q = jnp.where(q == 2, y, q)
+            at = pl.ds(pl.multiple_of(piece * PIECE, PIECE), PIECE)
+            similar = lax.dot_general(
+                buf[u, 0, at, :], buf[v, q], (((1,), (1,)), ((), ())), preferred_element_type=jnp.float32
+            )
+            shift = jnp.where((u == OWN) & (v == OWN) & (q == 0), piece * PIECE, 2 * rows)
+            row_ids = lax.broadcasted_iota(jnp.int32, similar.shape, 0)
+            col_ids = lax.broadcasted_iota(jnp.int32, similar.shape, 1)
+            similar = jnp.where(col_ids - row_ids == shift, lowest, similar)
+            best = row_acc[u, at]
+            for j in range(rows // LANES):
+                best = jnp.maximum(best, similar[:, j * LANES:(j + 1) * LANES])
+            row_acc[u, at] = best
+            tall = jnp.max(similar.reshape(PIECE // SUBLANES, SUBLANES, rows), axis=0)
+            col_acc[v, q] = jnp.maximum(col_acc[v, q], tall)
+
+    steps = len(waits)
+    numbers = [0] * 4
+    started = [[] for _ in range(4)]
+    for t in range(steps):
+        if t == 1:
+            side_copy(0).wait_recv()
+        if t == share + 1:
+            side_copy(1).wait_recv()
+        for p in range(4):
+
+            @pl.when(place == p)
+            def _():
+                early = [s for s in sends[t][p] if (s[1], s[3]) not in waits[t][p]]
+                for send in early:
+                    link_copy(*send, numbers[p]).start()
+                    started[p].append((*send, numbers[p]))
+                    numbers[p] += 1
+                for slot, c in waits[t][p]:
+                    arrival(slot, c).wait_recv()
+                    for send in sends[t][p]:
+                        if (send[1], send[3]) == (slot, c):
+                            link_copy(*send, numbers[p]).start()
+                            started[p].append((*send, numbers[p]))
+                            numbers[p] += 1
+
+        if t == 0:
+            side_copy(0).start()
+            row_acc[...] = jnp.full(row_acc.shape, lowest, jnp.float32)
+            col_acc[...] = jnp.full(col_acc.shape, lowest, jnp.float32)
+        if t == share:
+            side_copy(1).start()
+        multiply(work[t])
+    multiply(work[steps])
+
+    for slot in range(TOP + 1):
+
+        def fold(slot=slot):
+            across = jnp.max(jnp.transpose(row_acc[slot]), axis=0, keepdims=True)
+            if slot <= YNB:
+                down = [jnp.max(col_acc[slot, q], axis=0, keepdims=True) for q in range(2)]
+                parts[slot, 0] = jnp.maximum(across, down[0])
+                parts[slot, 1] = down[1]
+            else:
+                parts[slot, 0] = across
+
+        if min(OWNER[slot]) >= 0:
+            fold()
+        else:
+            pl.when(present(OWNER[slot], place))(fold)
+
+    def part_copy(slot, p, q):
+        n = 2 * slot + q
+        dy = 1 if slot == YNB else 0
+        return pltpu.make_async_remote_copy(
+            src_ref=parts.at[slot, q],
+            dst_ref=got.at[p, dy, q],
+            send_sem=part_send.at[n],
+            recv_sem=part_recv.at[p, dy, q],
+            device_id=device_at(OWNER[slot][p], dy, q),
+            device_id_type=MESH,
+        )
+
+    def messages(p):
+        result = [(OWN, 1), (YNB, 0), (YNB, 1)]
+        return result + [(slot, 0) for slot in (LOW, FAR, TOP) if OWNER[slot][p] >= 0]
+
+    for p in range(4):
+
+        @pl.when(place == p)
+        def _():
+            for slot, q in messages(p):
+                part_copy(slot, p, q).start()
+
+    o_ref[...] = parts[OWN, 0]
+    for p in range(4):
+
+        @pl.when(place == p)
+        def _():
+            sources = []
+            for sender in range(4):
+                for slot, q in messages(sender):
+                    if OWNER[slot][sender] == p:
+                        sources.append((sender, 1 if slot == YNB else 0, q))
+                        part_copy(slot, sender, q).wait_recv()
+            best = o_ref[...]
+            for source in sources:
+                best = jnp.maximum(best, got[source])
+            o_ref[...] = best
+            for slot, q in messages(p):
+                part_copy(slot, p, q).wait_send()
+            for way, slot, to, c, n in started[p]:
+                link_copy(way, slot, to, c, n).wait_send()
+
+    for n in range(2):
+        side_copy(n).wait_send()
+
+
+def present(table, index):
+    return pick([int(v >= 0) for v in table], index) == 1
+
+
+def relayed(embeddings):
+    rows, width = embeddings.shape
+    best = pl.pallas_call(
+        relay_kernel,
+        out_shape=jax.ShapeDtypeStruct((1, rows), jnp.float32),
+        in_specs=[pl.BlockSpec(memory_space=pltpu.VMEM)],
+        out_specs=pl.BlockSpec(memory_space=pltpu.VMEM),
+        scratch_shapes=[
+            pltpu.VMEM((BACK + 1, 2, rows, width), jnp.bfloat16),
+            pltpu.VMEM((TOP + 1, rows, LANES), jnp.float32),
+            pltpu.VMEM((2, 2, SUBLANES, rows), jnp.float32),
+            pltpu.VMEM((TOP + 1, 2, 1, rows), jnp.float32),
+            pltpu.VMEM((4, 2, 2, 1, rows), jnp.float32),
+            pltpu.SemaphoreType.DMA((64,)),
+            pltpu.SemaphoreType.DMA((BACK + 1, CHUNKS)),
+            pltpu.SemaphoreType.DMA((2,)),
+            pltpu.SemaphoreType.DMA((2,)),
+            pltpu.SemaphoreType.DMA((2 * TOP + 2,)),
+            pltpu.SemaphoreType.DMA((4, 2, 2)),
+        ],
+        compiler_params=pltpu.CompilerParams(
+            collective_id=1, has_side_effects=True, vmem_limit_bytes=48 * 2 ** 20
+        ),
+    )(embeddings)
+    return best.reshape(rows)
+
+
 def shards(embeddings, pair_list, pair_count):
     chips, cols = lax.axis_size("rows"), lax.axis_size("cols")
     rows, width = embeddings.shape
+    if (lax.axis_size("groups"), chips, cols) == (2, 8, 2):
+        return relayed(embeddings)
     plan = Plan(chips)
     unit = rows // plan.parts
     total = chips * cols

time: 69.9 us -> 73.5 us (1.052)
  Pallas kernels: 68 us -> 71.5 us
    pallas_call x1, Pallas kernels: 68 us -> 71.5 us  [relayed(): pl.pallas_call(relay_kernel, out_shape=jax.ShapeDtypeStruct((1, rows), jn...]
where the time goes in v2:
time: 73.5 us; the launch traced here: 73.3 us
  Pallas kernels  71.5 us (97%)
  local copies, waits for them, and re-layouts  1.8 us (2%)
    pallas_call x1, Pallas kernels, relayed(): pl.pallas_call(relay_kernel, out_shape=jax.ShapeDtypeStruct((1, rows), jn...  71.5 us
    unnamed x3, local copies, waits for them, and re-layouts  1.8 us

profile of v2, /device:TPU:0, one launch (start us, length us, event | category | flops | bytes accessed | tf_op | source)
XLA Modules:
  0.0 73.3 jit_solution(5276194877001293524)
XLA Ops:
  0.0 0.0 copy-start
  0.0 1.2 %copy-done = bf16[512,1024]{1,0:T(8,128)(2,1)S(1)} copy-done((bf16[512,1024]{1,0:T(8,128)(2,1)S(1)}, bf16[512,1024]{1,0:T(8,128)(2,1)}, u32[]{:S(2)}) %copy-start) | copy-done | bytes 1048600
  1.2 71.5 %shard_map.17 = f32[1,512]{1,0:T(1,128)S(1)} custom-call(bf16[512,1024]{1,0:T(8,128)(2,1)S(1)} %copy-done), custom_call_target="tpu_custom_call" | custom-call | tf_op jit(solution)/shard_map/pallas_call | solution.py:584
  72.8 0.6 copy.3
Async XLA Ops:
  0.0 1.2 %copy-start = (bf16[512,1024]{1,0:T(8,128)(2,1)S(1)}, bf16[512,1024]{1,0:T(8,128)(2,1)}, u32[]{:S(2)}) copy-start(bf16[512,1024]{1,0:T(8,128)(2,1)} %x_ref.1) | copy-start | bytes 3145732

commit v3 on v2

--- a/solution.py
+++ b/solution.py
@@ -282,25 +282,28 @@
 
 OWN, YNB, LOW, FAR, TOP, PASS, BACK = range(7)
 CHUNKS = 8
-PIECE = 128
-ALL, FIRST, SECOND = range(CHUNKS), range(CHUNKS // 2), range(CHUNKS // 2, CHUNKS)
-A_ORDER = list(SECOND) + list(FIRST)
+PIECE = 256
+ALL = range(CHUNKS)
+HERE, ROUND = range(5 * CHUNKS // 8), range(5 * CHUNKS // 8, CHUNKS)
 ROUTES = {
-    (0, OWN): [("x", PASS, A_ORDER), ("u", LOW, ALL), ("y", YNB, ALL)],
-    (1, OWN): [("u", LOW, ALL), ("y", YNB, ALL)],
+    (0, OWN): [("x", PASS, ROUND), ("u", LOW, ALL), ("y", YNB, ALL)],
+    (1, OWN): [("x", BACK, ROUND), ("u", LOW, HERE), ("y", YNB, ALL)],
     (2, OWN): [("y", YNB, ALL)],
-    (3, OWN): [("x", BACK, SECOND), ("d", TOP, FIRST), ("y", YNB, ALL)],
-    (3, PASS): [("d", PASS, ALL)],
-    (2, PASS): [("d", PASS, ALL)],
-    (1, PASS): [("x", FAR, ALL), ("d", PASS, SECOND)],
-    (0, PASS): [("x", FAR, SECOND)],
-    (0, BACK): [("u", BACK, SECOND)],
-    (1, BACK): [("x", TOP, SECOND)],
-    (2, LOW): [("u", LOW, ALL)],
-    (2, FAR): [("u", FAR, FIRST)],
+    (3, OWN): [("d", TOP, ALL), ("y", YNB, ALL)],
+    (3, PASS): [("d", PASS, ROUND)],
+    (2, PASS): [("d", PASS, ROUND)],
+    (1, PASS): [("x", FAR, ROUND), ("d", PASS, ROUND)],
+    (0, PASS): [("x", FAR, ROUND)],
+    (2, BACK): [("d", BACK, ROUND)],
+    (1, BACK): [("x", LOW, ROUND), ("d", BACK, ROUND)],
+    (0, BACK): [("x", LOW, ROUND)],
+    (1, LOW): [("u", FAR, HERE)],
+    (2, LOW): [("u", LOW, HERE)],
+    (2, FAR): [("u", FAR, HERE)],
 }
 OWNER = {OWN: [0, 1, 2, 3], YNB: [0, 1, 2, 3], LOW: [-1, 0, 1, 1], FAR: [-1, -1, 0, 0], TOP: [-1, -1, 3, -1]}
 BUDGET = 6
+AHEAD = 2
 
 
 def target(place, way):
@@ -342,7 +345,7 @@
                 item = min(queue)
                 queue.remove(item)
                 _, _, slot, to, c, ready = item
-                sends[max(ready, step - 1)][p].append((way, slot, to, c))
+                sends[max(ready, step - AHEAD)][p].append((way, slot, to, c))
                 landing.append((target(p, way), to, c))
         step += 1
     steps = len(waits)
@@ -350,7 +353,6 @@
     work = [[[] for _ in range(4)] for _ in range(steps + 1)]
     for p in range(4):
         jobs = []
-        pieces = range(2)
 
         def ready(slot, piece):
             per = CHUNKS // PIECES
@@ -364,8 +366,6 @@
                     at = ready(slot, piece)
                     jobs += [(max(1, at), (slot, piece, OWN, q)) for q in range(2)]
                     jobs += [(max(share + 1, at), (slot, piece, YNB, q)) for q in range(2)]
-        if p == 0:
-            jobs = [j for j in jobs]
         jobs.sort()
         for t in range(steps + 1):
             able = [j for j in jobs if j[0] <= t]
@@ -404,11 +404,16 @@
         return {"groups": group, "rows": 2 * zz + (y + dy) % 2, "cols": (core + q) % 2}
 
     barrier = pltpu.get_barrier_semaphore()
-    everyone = [(k, q) for k in range(8) for q in range(2) if (k, q) != (0, 0)]
-    pl.semaphore_signal(barrier, inc=1, device_id=neighbour("x"), device_id_type=MESH)
-    for k, q in everyone:
-        other = {"groups": group, "rows": (line + k) % 8, "cols": (core + q) % 2}
+    sibling = {"groups": group, "rows": line, "cols": 1 - core}
+
+    def greet(other):
         pl.semaphore_signal(barrier, inc=1, device_id=other, device_id_type=MESH)
+
+    greet(neighbour("x"))
+    greet(neighbour("y"))
+    greet(sibling)
+    pl.when(place < 3)(lambda: greet(neighbour("u")))
+    pl.when(place > 0)(lambda: greet(neighbour("d")))
 
     @pl.loop(0, CHUNKS)
     def _(c):
@@ -417,7 +422,7 @@
         mean = jnp.mean(values * values, axis=1, keepdims=True)
         buf[OWN, 0, at, :] = (values * lax.rsqrt(mean + epsilon) * width ** (-0.5)).astype(jnp.bfloat16)
 
-    pl.semaphore_wait(barrier, len(everyone) + 1)
+    pl.semaphore_wait(barrier, pick([4, 5, 5, 4], place))
 
     def link_copy(way, slot, to, c, n):
         at = pl.ds(c * chunk_rows, chunk_rows)
@@ -440,7 +445,7 @@
             dst_ref=buf.at[slot, 1],
             send_sem=side_send.at[n],
             recv_sem=side_recv.at[n],
-            device_id={"groups": group, "rows": line, "cols": 1 - core},
+            device_id=sibling,
             device_id_type=MESH,
         )
 
@@ -465,18 +470,18 @@
             q = jnp.where(q == 2, y, q)
             at = pl.ds(pl.multiple_of(piece * PIECE, PIECE), PIECE)
             similar = lax.dot_general(
-                buf[u, 0, at, :], buf[v, q], (((1,), (1,)), ((), ())), preferred_element_type=jnp.float32
+                buf[v, q], buf[u, 0, at, :], (((1,), (1,)), ((), ())), preferred_element_type=jnp.float32
             )
             shift = jnp.where((u == OWN) & (v == OWN) & (q == 0), piece * PIECE, 2 * rows)
             row_ids = lax.broadcasted_iota(jnp.int32, similar.shape, 0)
             col_ids = lax.broadcasted_iota(jnp.int32, similar.shape, 1)
-            similar = jnp.where(col_ids - row_ids == shift, lowest, similar)
-            best = row_acc[u, at]
-            for j in range(rows // LANES):
+            similar = jnp.where(row_ids - col_ids == shift, lowest, similar)
+            best = row_acc[v, q]
+            for j in range(PIECE // LANES):
                 best = jnp.maximum(best, similar[:, j * LANES:(j + 1) * LANES])
-            row_acc[u, at] = best
-            tall = jnp.max(similar.reshape(PIECE // SUBLANES, SUBLANES, rows), axis=0)
-            col_acc[v, q] = jnp.maximum(col_acc[v, q], tall)
+            row_acc[v, q] = best
+            tall = jnp.max(similar.reshape(rows // SUBLANES, SUBLANES, PIECE), axis=0)
+            col_acc[u, :, at] = jnp.maximum(col_acc[u, :, at], tall)
 
     steps = len(waits)
     numbers = [0] * 4
@@ -515,13 +520,13 @@
     for slot in range(TOP + 1):
 
         def fold(slot=slot):
-            across = jnp.max(jnp.transpose(row_acc[slot]), axis=0, keepdims=True)
+            down = jnp.max(col_acc[slot], axis=0, keepdims=True)
             if slot <= YNB:
-                down = [jnp.max(col_acc[slot, q], axis=0, keepdims=True) for q in range(2)]
-                parts[slot, 0] = jnp.maximum(across, down[0])
-                parts[slot, 1] = down[1]
+                across = [jnp.max(jnp.transpose(row_acc[slot, q]), axis=0, keepdims=True) for q in range(2)]
+                parts[slot, 0] = jnp.maximum(across[0], down)
+                parts[slot, 1] = across[1]
             else:
-                parts[slot, 0] = across
+                parts[slot, 0] = down
 
         if min(OWNER[slot]) >= 0:
             fold()
@@ -588,8 +593,8 @@
         out_specs=pl.BlockSpec(memory_space=pltpu.VMEM),
         scratch_shapes=[
             pltpu.VMEM((BACK + 1, 2, rows, width), jnp.bfloat16),
-            pltpu.VMEM((TOP + 1, rows, LANES), jnp.float32),
-            pltpu.VMEM((2, 2, SUBLANES, rows), jnp.float32),
+            pltpu.VMEM((2, 2, rows, LANES), jnp.float32),
+            pltpu.VMEM((TOP + 1, SUBLANES, rows), jnp.float32),
             pltpu.VMEM((TOP + 1, 2, 1, rows), jnp.float32),
             pltpu.VMEM((4, 2, 2, 1, rows), jnp.float32),
             pltpu.SemaphoreType.DMA((64,)),

time: 73.5 us -> 54.6 us (0.74)
  Pallas kernels: 71.5 us -> 52.7 us
    pallas_call x1, Pallas kernels: 71.5 us -> 52.7 us  [relayed(): pl.pallas_call(relay_kernel, out_shape=jax.ShapeDtypeStruct((1, rows), jn...]
where the time goes in v3:
time: 54.6 us; the launch traced here: 54.5 us
  Pallas kernels  52.7 us (97%)
  local copies, waits for them, and re-layouts  1.8 us (3%)
    pallas_call x1, Pallas kernels, relayed(): pl.pallas_call(relay_kernel, out_shape=jax.ShapeDtypeStruct((1, rows), jn...  52.7 us
    unnamed x3, local copies, waits for them, and re-layouts  1.8 us

profile of v3, /device:TPU:0, one launch (start us, length us, event | category | flops | bytes accessed | tf_op | source)
XLA Modules:
  0.0 54.5 jit_solution(18416479229312355841)
XLA Ops:
  0.0 0.0 copy-start
  0.0 1.2 %copy-done = bf16[512,1024]{1,0:T(8,128)(2,1)S(1)} copy-done((bf16[512,1024]{1,0:T(8,128)(2,1)S(1)}, bf16[512,1024]{1,0:T(8,128)(2,1)}, u32[]{:S(2)}) %copy-start) | copy-done | bytes 1048600
  1.2 52.7 %shard_map.17 = f32[1,512]{1,0:T(1,128)S(1)} custom-call(bf16[512,1024]{1,0:T(8,128)(2,1)S(1)} %copy-done), custom_call_target="tpu_custom_call" | custom-call | tf_op jit(solution)/shard_map/pallas_call | solution.py:589
  53.9 0.6 %copy.3 = f32[512]{0:T(512)} copy(f32[512]{0:T(512)S(1)} %bitcast.1) | data formatting | bytes 4096
Async XLA Ops:
  0.0 1.2 %copy-start = (bf16[512,1024]{1,0:T(8,128)(2,1)S(1)}, bf16[512,1024]{1,0:T(8,128)(2,1)}, u32[]{:S(2)}) copy-start(bf16[512,1024]{1,0:T(8,128)(2,1)} %x_ref.1) | copy-start | bytes 3145732

commit v4 on v3

--- a/solution.py
+++ b/solution.py
@@ -302,7 +302,7 @@
     (2, FAR): [("u", FAR, HERE)],
 }
 OWNER = {OWN: [0, 1, 2, 3], YNB: [0, 1, 2, 3], LOW: [-1, 0, 1, 1], FAR: [-1, -1, 0, 0], TOP: [-1, -1, 3, -1]}
-BUDGET = 6
+BUDGET = 4
 AHEAD = 2
 
 
@@ -359,13 +359,13 @@
             return max(arrived[p, slot, c] for c in range(piece * per, piece * per + per))
 
         for piece in range(PIECES):
-            jobs += [(1, (OWN, piece, OWN, q)) for q in range(2)]
-            jobs.append((share + 1, (OWN, piece, YNB, 2)))
+            jobs.append((1, (OWN, piece, OWN, 0)))
             for slot in (LOW, FAR, TOP):
                 if OWNER[slot][p] >= 0:
                     at = ready(slot, piece)
-                    jobs += [(max(1, at), (slot, piece, OWN, q)) for q in range(2)]
-                    jobs += [(max(share + 1, at), (slot, piece, YNB, q)) for q in range(2)]
+                    jobs.append((max(1, at), (slot, piece, OWN, 0)))
+                    jobs.append((max(share + 1, at), (slot, piece, YNB, 0)))
+        jobs.append((share + 1, (OWN, 0, YNB, 1)))
         jobs.sort()
         for t in range(steps + 1):
             able = [j for j in jobs if j[0] <= t]
@@ -380,9 +380,11 @@
 
 
 def relay_kernel(
-    x_ref, o_ref, buf, row_acc, col_acc, parts, got,
-    send_sem, recv_sem, side_send, side_recv, part_send, part_recv,
+    x_hbm, o_ref, x_ref, buf, row_acc, col_acc, parts, got,
+    load_sem, send_sem, recv_sem, side_send, side_recv, part_send, part_recv,
 ):
+    load = pltpu.make_async_copy(x_hbm, x_ref, load_sem)
+    load.start()
     waits, sends, work, share = relay_plan()
     group, line, core = lax.axis_index("groups"), lax.axis_index("rows"), lax.axis_index("cols")
     z, y = line // 2, line % 2
@@ -414,6 +416,8 @@
     greet(sibling)
     pl.when(place < 3)(lambda: greet(neighbour("u")))
     pl.when(place > 0)(lambda: greet(neighbour("d")))
+
+    load.wait()
 
     @pl.loop(0, CHUNKS)
     def _(c):
@@ -467,21 +471,24 @@
                 word = jnp.where(n >= 3 * k, words[k], word)
             word = word >> (9 * (n % 3))
             u, piece, v, q = word & 7, (word >> 3) & 7, (word >> 6) & 1, (word >> 7) & 3
-            q = jnp.where(q == 2, y, q)
+            shared = q == 1
+            u, piece, v = jnp.where(shared, y, u), jnp.where(shared, y, piece), jnp.where(shared, 1 - y, v)
             at = pl.ds(pl.multiple_of(piece * PIECE, PIECE), PIECE)
-            similar = lax.dot_general(
-                buf[v, q], buf[u, 0, at, :], (((1,), (1,)), ((), ())), preferred_element_type=jnp.float32
-            )
-            shift = jnp.where((u == OWN) & (v == OWN) & (q == 0), piece * PIECE, 2 * rows)
-            row_ids = lax.broadcasted_iota(jnp.int32, similar.shape, 0)
-            col_ids = lax.broadcasted_iota(jnp.int32, similar.shape, 1)
-            similar = jnp.where(row_ids - col_ids == shift, lowest, similar)
-            best = row_acc[v, q]
-            for j in range(PIECE // LANES):
-                best = jnp.maximum(best, similar[:, j * LANES:(j + 1) * LANES])
-            row_acc[v, q] = best
-            tall = jnp.max(similar.reshape(rows // SUBLANES, SUBLANES, PIECE), axis=0)
-            col_acc[u, :, at] = jnp.maximum(col_acc[u, :, at], tall)
+            for plane in range(2):
+                similar = lax.dot_general(
+                    buf[v, plane], buf[u, 0, at, :], (((1,), (1,)), ((), ())), preferred_element_type=jnp.float32
+                )
+                if plane == 0:
+                    shift = jnp.where((u == OWN) & (v == OWN), piece * PIECE, 2 * rows)
+                    row_ids = lax.broadcasted_iota(jnp.int32, similar.shape, 0)
+                    col_ids = lax.broadcasted_iota(jnp.int32, similar.shape, 1)
+                    similar = jnp.where(row_ids - col_ids == shift, lowest, similar)
+                best = row_acc[v, plane]
+                for j in range(PIECE // LANES):
+                    best = jnp.maximum(best, similar[:, j * LANES:(j + 1) * LANES])
+                row_acc[v, plane] = best
+                tall = jnp.max(similar.reshape(rows // SUBLANES, SUBLANES, PIECE), axis=0)
+                col_acc[u, :, at] = jnp.maximum(col_acc[u, :, at], tall)
 
     steps = len(waits)
     numbers = [0] * 4
@@ -589,14 +596,16 @@
     best = pl.pallas_call(
         relay_kernel,
         out_shape=jax.ShapeDtypeStruct((1, rows), jnp.float32),
-        in_specs=[pl.BlockSpec(memory_space=pltpu.VMEM)],
+        in_specs=[pl.BlockSpec(memory_space=pl.ANY)],
         out_specs=pl.BlockSpec(memory_space=pltpu.VMEM),
         scratch_shapes=[
+            pltpu.VMEM((rows, width), jnp.bfloat16),
             pltpu.VMEM((BACK + 1, 2, rows, width), jnp.bfloat16),
             pltpu.VMEM((2, 2, rows, LANES), jnp.float32),
             pltpu.VMEM((TOP + 1, SUBLANES, rows), jnp.float32),
             pltpu.VMEM((TOP + 1, 2, 1, rows), jnp.float32),
             pltpu.VMEM((4, 2, 2, 1, rows), jnp.float32),
+            pltpu.SemaphoreType.DMA,
             pltpu.SemaphoreType.DMA((64,)),
             pltpu.SemaphoreType.DMA((BACK + 1, CHUNKS)),
             pltpu.SemaphoreType.DMA((2,)),

time: 54.6 us -> 52.8 us (0.967)
  Pallas kernels: 52.7 us -> 50.9 us
    pallas_call x1, Pallas kernels: 52.7 us -> 50.9 us  [relayed(): pl.pallas_call(relay_kernel, out_shape=jax.ShapeDtypeStruct((1, rows), jn...]
where the time goes in v4:
time: 52.8 us; the launch traced here: 52.7 us
  Pallas kernels  50.9 us (96%)
  local copies, waits for them, and re-layouts  1.8 us (3%)
    pallas_call x1, Pallas kernels, relayed(): pl.pallas_call(relay_kernel, out_shape=jax.ShapeDtypeStruct((1, rows), jn...  50.9 us
    unnamed x3, local copies, waits for them, and re-layouts  1.8 us

profile of v4, /device:TPU:0, one launch (start us, length us, event | category | flops | bytes accessed | tf_op | source)
XLA Modules:
  0.0 52.7 jit_solution(7956770421321014622)
XLA Ops:
  0.0 0.0 copy-start
  0.0 1.2 %copy-done = bf16[512,1024]{1,0:T(8,128)(2,1)S(1)} copy-done((bf16[512,1024]{1,0:T(8,128)(2,1)S(1)}, bf16[512,1024]{1,0:T(8,128)(2,1)}, u32[]{:S(2)}) %copy-start) | copy-done | bytes 1048600
  1.2 50.9 %shard_map.17 = f32[1,512]{1,0:T(1,128)S(1)} custom-call(bf16[512,1024]{1,0:T(8,128)(2,1)S(1)} %copy-done), custom_call_target="tpu_custom_call" | custom-call | tf_op jit(solution)/shard_map/pallas_call | solution.py:596
  52.1 0.6 %copy.3 = f32[512]{0:T(512)} copy(f32[512]{0:T(512)S(1)} %bitcast.1) | data formatting | bytes 4096
Async XLA Ops:
  0.0 1.2 %copy-start = (bf16[512,1024]{1,0:T(8,128)(2,1)S(1)}, bf16[512,1024]{1,0:T(8,128)(2,1)}, u32[]{:S(2)}) copy-start(bf16[512,1024]{1,0:T(8,128)(2,1)} %x_hbm.1) | copy-start | bytes 3145732

commit v5 on v4

--- a/solution.py
+++ b/solution.py
@@ -524,22 +524,6 @@
         multiply(work[t])
     multiply(work[steps])
 
-    for slot in range(TOP + 1):
-
-        def fold(slot=slot):
-            down = jnp.max(col_acc[slot], axis=0, keepdims=True)
-            if slot <= YNB:
-                across = [jnp.max(jnp.transpose(row_acc[slot, q]), axis=0, keepdims=True) for q in range(2)]
-                parts[slot, 0] = jnp.maximum(across[0], down)
-                parts[slot, 1] = across[1]
-            else:
-                parts[slot, 0] = down
-
-        if min(OWNER[slot]) >= 0:
-            fold()
-        else:
-            pl.when(present(OWNER[slot], place))(fold)
-
     def part_copy(slot, p, q):
         n = 2 * slot + q
         dy = 1 if slot == YNB else 0
@@ -556,12 +540,29 @@
         result = [(OWN, 1), (YNB, 0), (YNB, 1)]
         return result + [(slot, 0) for slot in (LOW, FAR, TOP) if OWNER[slot][p] >= 0]
 
-    for p in range(4):
-
-        @pl.when(place == p)
-        def _():
-            for slot, q in messages(p):
-                part_copy(slot, p, q).start()
+    for slot in (LOW, FAR, TOP, YNB, OWN):
+
+        def fold(slot=slot):
+            down = jnp.max(col_acc[slot], axis=0, keepdims=True)
+            if slot <= YNB:
+                across = [jnp.max(jnp.transpose(row_acc[slot, q]), axis=0, keepdims=True) for q in range(2)]
+                parts[slot, 0] = jnp.maximum(across[0], down)
+                parts[slot, 1] = across[1]
+            else:
+                parts[slot, 0] = down
+
+        if min(OWNER[slot]) >= 0:
+            fold()
+        else:
+            pl.when(present(OWNER[slot], place))(fold)
+        if slot in (TOP, YNB, OWN):
+            for p in range(4):
+
+                @pl.when(place == p)
+                def _():
+                    for item, q in messages(p):
+                        if item == slot or (slot == TOP and item > YNB):
+                            part_copy(item, p, q).start()
 
     o_ref[...] = parts[OWN, 0]
     for p in range(4):

time: 52.8 us -> 52.4 us (level)
  no operation moved by 1% of the time
where the time goes in v5:
time: 52.4 us; the launch traced here: 52.3 us
  Pallas kernels  50.5 us (96%)
  local copies, waits for them, and re-layouts  1.8 us (3%)
    pallas_call x1, Pallas kernels, relayed(): pl.pallas_call(relay_kernel, out_shape=jax.ShapeDtypeStruct((1, rows), jn...  50.5 us
    unnamed x3, local copies, waits for them, and re-layouts  1.8 us

profile of v5, /device:TPU:0, one launch (start us, length us, event | category | flops | bytes accessed | tf_op | source)
XLA Modules:
  0.0 52.3 jit_solution(15481321115378677989)
XLA Ops:
  0.0 0.0 copy-start
  0.0 1.2 %copy-done = bf16[512,1024]{1,0:T(8,128)(2,1)S(1)} copy-done((bf16[512,1024]{1,0:T(8,128)(2,1)S(1)}, bf16[512,1024]{1,0:T(8,128)(2,1)}, u32[]{:S(2)}) %copy-start) | copy-done | bytes 1048600
  1.2 50.5 %shard_map.17 = f32[1,512]{1,0:T(1,128)S(1)} custom-call(bf16[512,1024]{1,0:T(8,128)(2,1)S(1)} %copy-done), custom_call_target="tpu_custom_call" | custom-call | tf_op jit(solution)/shard_map/pallas_call | solution.py:597
  51.7 0.6 %copy.3 = f32[512]{0:T(512)} copy(f32[512]{0:T(512)S(1)} %bitcast.1) | data formatting | bytes 4096
Async XLA Ops:
  0.0 1.2 %copy-start = (bf16[512,1024]{1,0:T(8,128)(2,1)S(1)}, bf16[512,1024]{1,0:T(8,128)(2,1)}, u32[]{:S(2)}) copy-start(bf16[512,1024]{1,0:T(8,128)(2,1)} %x_hbm.1) | copy-start | bytes 3145732
